TPU v7x, 768 devices: a whole 4x8x12 slice. The times are simulated.
768 devices in a mesh: fault: 192 (over z, y, core), off: 4 (over x).
Axes of the slice: x: 4, y: 8, z: 12, core: 2. Of those that a mesh axis runs over, the one named last changes fastest.
Arguments:
- modal_state: float32 [9, 56, 24576], P(None, None, ('fault', 'off')), may hold values from -6 to 6
- star_mats: float32 [3, 9, 9, 24576], P(None, None, None, ('fault', 'off')), may hold values from -2 to 2
- flux_local: float32 [4, 9, 9, 24576], P(None, None, None, ('fault', 'off')), may hold values from -1 to 1
- flux_nbr: float32 [4, 9, 9, 24576], P(None, None, None, ('fault', 'off')), may hold values from -1 to 1
- stiff_time: float32 [3, 56, 56], replicated, may hold values from -0.75 to 0.75
- stiff_vol: float32 [3, 56, 56], replicated, may hold values from -0.375 to 0.375
- flux_minus: float32 [4, 56, 56], replicated, may hold values from -0.375 to 0.375
- face_proj: float32 [4, 56, 21], replicated, may hold values from -0.75 to 0.75
- face_turn: float32 [3, 21, 21], replicated, may hold values from -1.25 to 1.25
- face_lift: float32 [4, 21, 56], replicated, may hold values from -0.625 to 0.625
- cluster: int32 [24576], P(('fault', 'off')), may hold values from 0 to 1, as said below
- send_elem: int32 [192, 4, 72], P('fault', 'off'), may hold values from 0 to 31
- send_face: int32 [192, 4, 72], P('fault', 'off'), may hold values from 0 to 3
- nbr_index: int32 [4, 24576], P(None, ('fault', 'off')), may hold values from 0 to 199, as said below
- orientation: int32 [4, 24576], P(None, ('fault', 'off')), may hold values from 0 to 2
- source_elem: int32 [16], replicated, may hold values from 0 to 24575
- source_term: float32 [16, 9, 56], replicated, may hold values from -6 to 6
Outputs:
- new_state: float32 [9, 56, 24576], P(None, None, ('fault', 'off'))
Inputs may be any that keep to these rules, and one draw needn't show every extreme that they name: `cluster`: each device holds at most 16 fine elements, and some device exactly 16 in every draw. `nbr_index`: on each device, entries below 128 name the device's own face traces; every received entry 128 .. 199 is named by exactly one face of the device.
All inputs are finite; a program needn't handle non-finite values.
Results may differ from a plain program's by a relative error of at most 0.0003.
Values sent between devices are 32-bit elements; how exact they have to be, the bound alone decides.
A program may use at most 32 MiB of HBM per device.

v0:
```python
import functools
import math

import jax
import jax.numpy as jnp
import numpy as np
from jax import lax
from jax.experimental import pallas as pl
from jax.experimental.pallas import tpu as pltpu
from jax.sharding import PartitionSpec as P

TERMS = 6
HALF_STEP = 0.5
F32 = jnp.float32
BF16 = jnp.bfloat16
MESH = pl.DeviceIdType.MESH
Q = 9
M = 56
J = 21
E = 32
FINE = 16


def weights_over(start, finish):
    return [
        (finish ** (k + 1) - start ** (k + 1)) / math.factorial(k + 1) for k in range(TERMS)
    ]


def split2(x):
    hi = x.astype(BF16)
    return hi, (x - hi.astype(F32)).astype(BF16)


def split3(x):
    hi = x.astype(BF16)
    rest = x - hi.astype(F32)
    mid = rest.astype(BF16)
    return hi, mid, (rest - mid.astype(F32)).astype(BF16)


def dot(a, b):
    return jnp.dot(a, b, preferred_element_type=F32)


def dot_nt(a, b):
    return lax.dot_general(a, b, (((1,), (1,)), ((), ())), preferred_element_type=F32)


def iota(shape, axis):
    return lax.broadcasted_iota(jnp.int32, shape, axis)


def flag(mask):
    return jnp.where(mask, 1.0, 0.0).astype(F32)


def spread_tables():
    lane = np.arange(256)
    star = np.stack([(lane // 64 == 0), (lane // 64 == 1), (lane // 64 >= 2), lane < 0])
    own = np.stack([lane // 64 == f for f in range(4)])
    nbr = np.stack([lane[:128] // 32 == f for f in range(4)])

    def table(pattern):
        width = pattern.shape[1]
        out = np.zeros((4, 2, 4, 4, 8, width), np.float32)
        for i in range(4):
            out[i, :, :, i, :4, :] = pattern
        return out.reshape(4, 256, width)

    return [jnp.asarray(table(t), BF16) for t in (star, own, nbr)]


def kernel(
    n_fault,
    n_off,
    modal_h,
    star_h,
    own_h,
    nbr_h,
    st_h,
    sv_h,
    fm_h,
    proj_h,
    turn_h,
    lift_h,
    cluster_h,
    send_elem_h,
    send_face_h,
    index_h,
    orient_h,
    src_elem_h,
    src_term_h,
    bh_star_h,
    bh_own_h,
    bh_nbr_h,
    out_ref,
    modal,
    star8,
    own8,
    nbr8,
    st,
    sv,
    fm,
    proj,
    turn,
    lift,
    cluster,
    send_elem,
    send_face,
    index,
    orient,
    src_elem,
    src_term,
    bh_star,
    bh_own,
    bh_nbr,
    cs,
    cs2,
    co,
    cn,
    spread_lhs,
    wt32,
    wt,
    wu32,
    wu,
    pw32,
    pw_hi,
    pw_lo,
    state0,
    term,
    first,
    second,
    half,
    later,
    part,
    near1,
    gather_loc,
    gather_rem,
    gather_out,
    rhs,
    send1,
    send2,
    recv1,
    recv2,
    in_sems,
    send_sems,
    recv_sems,
):
    fault = lax.axis_index("fault")
    off = lax.axis_index("off")
    below = lax.rem(fault + n_fault - 1, n_fault)
    above = lax.rem(fault + 1, n_fault)

    star8[...] = jnp.zeros_like(star8)
    own8[...] = jnp.zeros_like(own8)
    nbr8[...] = jnp.zeros_like(nbr8)
    pairs = [
        (cluster_h, cluster),
        (star_h, star8.at[0:81, 0:3, :]),
        (bh_star_h, bh_star),
        (modal_h, modal),
        (st_h, st),
        (index_h, index),
        (send_elem_h, send_elem),
        (send_face_h, send_face),
        (proj_h, proj),
        (own_h, own8.at[0:81, 0:4, :]),
        (bh_own_h, bh_own),
        (sv_h, sv),
        (fm_h, fm),
        (nbr_h, nbr8.at[0:81, 0:4, :]),
        (bh_nbr_h, bh_nbr),
        (orient_h, orient),
        (turn_h, turn),
        (lift_h, lift),
        (src_elem_h, src_elem),
        (src_term_h, src_term),
    ]
    copies = []
    for i, (src, dst) in enumerate(pairs):
        copies.append(pltpu.make_async_copy(src, dst, in_sems.at[i]))
        copies[-1].start()

    barrier = pltpu.get_barrier_semaphore()
    for device in [{"fault": below}, {"fault": above}]:
        pl.semaphore_signal(barrier, inc=1, device_id=device, device_id_type=MESH)
    for step in range(1, n_off):
        pl.semaphore_signal(
            barrier,
            inc=1,
            device_id={"off": lax.rem(off + step, n_off)},
            device_id_type=MESH,
        )

    low_half = iota((16, 128), 1) < 64

    wt32[...] = jnp.zeros_like(wt32)
    wu32[...] = jnp.zeros_like(wu32)
    pw32[...] = jnp.zeros_like(pw32)

    def wait(*which):
        for i in which:
            copies[i].wait()

    wait(0)
    row32 = iota((32, 128), 0)
    lane32 = iota((32, 128), 1)
    col = lane32 & 31
    fine_row = jnp.broadcast_to(cluster[...].astype(F32), (16, 32)).astype(BF16)
    cum = dot(fine_row, flag(row32 <= col).astype(BF16))
    fine4 = dot(fine_row, flag(row32 == col).astype(BF16))
    n_fine = dot(fine_row, jnp.ones((32, 128), BF16))
    col16 = iota((16, 128), 1) & 31
    pos = jnp.where(fine4 > 0.5, cum - 1.0, n_fine + col16.astype(F32) - cum)
    pos = pos.astype(jnp.int32)[0:1]
    is_fine = iota((16, 128), 0).astype(F32) < n_fine
    perm = flag(iota((32, 32), 0) == pos[:, 0:32]).astype(BF16)
    row128 = iota((128, 128), 0)
    lane128 = iota((128, 128), 1)
    perm_big = flag(((row128 >> 5) == (lane128 >> 5)) & ((row128 & 31) == pos)).astype(BF16)

    def spread(rows, table, out, width):
        flat = rows[...].reshape(84 * 8, 32)
        hi, lo = split2(flat)
        g_hi = dot_nt(perm, hi).astype(BF16)
        g_lo = dot_nt(perm, lo).astype(BF16)
        lane = iota((32, 128), 1)
        for tile in range(6):
            hi_t = g_hi[:, 128 * tile : 128 * tile + 128] if tile < 5 else None
            lo_t = g_lo[:, 128 * tile : 128 * tile + 128] if tile < 5 else None
            if tile == 5:
                pad = jnp.zeros((32, 96), BF16)
                hi_t = jnp.concatenate([g_hi[:, 640:672], pad], axis=1)
                lo_t = jnp.concatenate([g_lo[:, 640:672], pad], axis=1)
            for c in range(4 if tile < 5 else 1):
                keep = flag((lane >> 5) == c).astype(BF16)
                chunk = 4 * tile + c
                spread_lhs[32 * chunk : 32 * chunk + 32, 0:128] = hi_t * keep
                spread_lhs[32 * chunk : 32 * chunk + 32, 128:256] = lo_t * keep

        def step(i, carry):
            out[i] = dot(spread_lhs[...], table[i]).reshape(21, 32, width)
            return carry

        lax.fori_loop(0, 4, step, 0)

    wait(1, 2)
    spread(star8, bh_star, cs, 256)

    def coef(table, q, p, rows, lanes):
        qp = Q * q + p
        return table[qp % 4, qp // 4, rows, lanes]

    low32 = iota((32, 128), 1) < 64
    upper = slice(128, 256)
    lower = slice(0, 128)
    whole = slice(0, 32)
    for q in range(Q):
        for pair in range(5):
            a = coef(cs, q, 2 * pair, whole, upper)
            b = coef(cs, q, 2 * pair + 1, whole, upper) if pair < 4 else 0.0
            cs2[q, pair] = jnp.where(low32, a, b)

    wait(4)
    for d in range(4):
        w = st[min(d, 2)]
        wt32[64 * d : 64 * d + M, 0:M] = w
        wt32[64 * d : 64 * d + M, 64 : 64 + M] = w
    w_hi, w_lo = split2(wt32[...])
    wt[:, 0:128] = w_hi
    wt[:, 128:256] = w_lo

    wait(3)
    term[...] = jnp.zeros_like(term)
    for q in range(Q):
        term[q, :, 0:M] = modal[q]
        term[q, :, 64 : 64 + M] = modal[q]
    perm3 = jnp.concatenate([perm, perm, perm], axis=1)
    early = weights_over(0.0, HALF_STEP)
    late = weights_over(HALF_STEP, 1.0)
    for q in range(Q):
        moved = dot(perm3, jnp.concatenate(split3(term[q]), axis=0))
        state0[q] = moved
        term[q] = moved
        first[q] = early[0] * moved
        second[q] = late[0] * moved

    def paired(xs):
        return [jnp.where(low_half, xs[2 * i], xs[2 * i + 1]) for i in range(4)] + [xs[8]]

    def mix_star(xs, xp, q, rows):
        y01 = coef(cs, q, 0, rows, lower) * xs[0]
        for p in range(1, Q):
            y01 = y01 + coef(cs, q, p, rows, lower) * xs[p]
        y2 = cs2[q, 0, rows, :] * xp[0]
        for i in range(1, 5):
            y2 = y2 + cs2[q, i, rows, :] * xp[i]
        return y01, y2

    def product(blocks, weights):
        his, los = [], []
        for row in blocks:
            cut = [split2(b) for b in row]
            his.append(jnp.concatenate([c[0] for c in cut], axis=1))
            los.append(jnp.concatenate([c[1] for c in cut], axis=1))
        both = dot(jnp.concatenate(his, axis=0), weights)
        extra = dot(jnp.concatenate(los, axis=0), weights[:, 0:128])
        return both[:, 0:128] + both[:, 128:256] + extra

    def series_weight(k, values):
        w = jnp.float32(values[TERMS - 1])
        for i in range(1, TERMS - 1):
            w = jnp.where(k == i, jnp.float32(values[i]), w)
        return w

    def predict(halves, sums):
        def step(k, carry):
            for h in range(halves):
                rows = slice(16 * h, 16 * h + 16)
                xs = [term[p, rows, :] for p in range(Q)]
                xp = paired(xs)
                blocks = [list(mix_star(xs, xp, q, rows)) for q in range(Q)]
                made = product(blocks, wt[...])
                for q in range(Q):
                    x = made[16 * q : 16 * q + 16]
                    term[q, rows, :] = x
                    for ref, values in sums:
                        ref[q, rows, :] = ref[q, rows, :] + series_weight(k, values) * x
            return carry

        lax.fori_loop(1, TERMS, step, 0)

    predict(2, [(first, early), (second, late)])

    wait(5, 6, 7)
    tab = iota((128, 32), 0)
    slot = tab & 15
    ghost = jnp.where(
        tab < 32,
        128 + tab,
        jnp.where((slot < 10) & (tab < 96), 160 + 10 * ((tab >> 4) - 2) + slot, -1),
    )
    for f in range(4):
        want = index[f : f + 1, :]
        loc = dot_nt(perm, flag(tab == want).astype(BF16)).astype(BF16)
        loc = dot_nt(loc, perm_big).astype(BF16)
        rem = dot_nt(perm, flag(ghost == want).astype(BF16)).astype(BF16)
        rows = slice(32 * f, 32 * f + 32)
        gather_loc[rows, 0:128] = loc
        gather_loc[rows, 128:256] = loc
        gather_rem[rows, 0:128] = rem
        gather_rem[rows, 128:256] = rem
    wanted = send_face[...] * E + send_elem[...]
    out_hot = flag(iota((128, 72), 0) == wanted).astype(BF16)
    r = iota((96, 72), 0)
    s = iota((96, 72), 1)
    k_in = r & 15
    slot_of = jnp.where(r < 32, r, jnp.where(k_in < 10, 32 + 10 * ((r >> 4) - 2) + k_in, -1))
    picked = dot_nt(flag(slot_of == s).astype(BF16), out_hot).astype(BF16)
    picked = dot_nt(picked, perm_big).astype(BF16)
    gather_out[:, 0:128] = picked
    gather_out[:, 128:256] = picked

    wait(8)
    for f in range(4):
        face = proj[:, f, :]
        for g in range(4):
            start = 128 * f + 32 * g
            pw32[start : start + J, 64 * g : 64 * g + M] = face
    p_hi, p_lo = split2(pw32[...])
    pw_hi[...] = p_hi
    pw_lo[...] = p_lo

    def make_table(integral):
        rows = []
        xs = [integral[q] for q in range(Q)]
        for k in range(2):
            a, b, c, d = xs[4 * k : 4 * k + 4]
            rows.append(
                jnp.concatenate([jnp.where(low32, a, b), jnp.where(low32, c, d)], axis=1)
            )
        rows.append(
            jnp.concatenate([jnp.where(low32, xs[8], 0.0), jnp.zeros((32, 128), F32)], axis=1)
        )
        hi, lo = split2(jnp.concatenate(rows, axis=0))
        faced = dot_nt(hi, pw_hi[...]) + dot_nt(hi, pw_lo[...]) + dot_nt(lo, pw_hi[...])
        for k in range(3):
            for f in range(4):
                t_hi, t_lo = split2(faced[32 * k : 32 * k + 32, 128 * f : 128 * f + 128])
                lanes = slice(128 * k, 128 * k + 128)
                rhs[32 * f : 32 * f + 32, lanes] = t_hi
                rhs[128 + 32 * f : 160 + 32 * f, lanes] = t_lo

    def exchange(sent, received, turn_no):
        outgoing = dot(gather_out[...], rhs[...])
        for a in range(6):
            for k in range(3):
                sent[pl.ds(48 * a + k, 16, stride=3), :] = outgoing[
                    16 * a : 16 * a + 16, 128 * k : 128 * k + 128
                ]
        started = []
        for a, device in enumerate([{"fault": below}, {"fault": above}]):
            started.append(
                pltpu.make_async_remote_copy(
                    src_ref=sent.at[pl.ds(48 * a, 48), :],
                    dst_ref=received.at[1 - a],
                    send_sem=send_sems.at[turn_no, a],
                    recv_sem=recv_sems.at[turn_no, 1 - a],
                    device_id=device,
                    device_id_type=MESH,
                )
            )
            started[-1].start()
        for step in range(1, n_off):
            to = lax.rem(off + step, n_off)
            started.append(
                pltpu.make_async_remote_copy(
                    src_ref=sent.at[pl.ds(pl.multiple_of(96 + 48 * to, 8), 32), :],
                    dst_ref=received.at[2 + off, pl.ds(0, 32), :],
                    send_sem=send_sems.at[turn_no, 1 + step],
                    recv_sem=recv_sems.at[turn_no, 1 + step],
                    device_id={"off": to},
                    device_id_type=MESH,
                )
            )
            started[-1].start()
        received[2 + off] = sent[pl.ds(pl.multiple_of(96 + 48 * off, 8), 48), :]
        return started

    def arrived(started, received):
        for copy in started:
            copy.wait()
        few = iota((16, 128), 0) < 10
        for k in range(3):
            lanes = slice(128 * k, 128 * k + 128)
            for a in range(6):
                piece = received[a, pl.ds(k, 16, stride=3), :]
                if a >= 2:
                    piece = jnp.where(few, piece, 0.0)
                hi, lo = split2(piece)
                rhs[16 * a : 16 * a + 16, lanes] = hi
                rhs[128 + 16 * a : 144 + 16 * a, lanes] = lo
            rhs[96:128, lanes] = jnp.zeros((32, 128), BF16)
            rhs[224:256, lanes] = jnp.zeros((32, 128), BF16)
        return dot(gather_rem[...], rhs[...])

    group = iota((16, 128), 1) >> 5

    def faces_of(near, h):
        made = []
        turned = {}
        for k in range(3):
            for f in range(4):
                base = near(f, k)
                turned[f, k, 0] = base
                shifts = range(1, 4) if k < 2 else [f] if f else []
                for shift in shifts:
                    turned[f, k, shift] = pltpu.roll(base, 32 * shift, 1)
        for q in range(Q):
            k, g = q // 4, q % 4
            out = turned[3, k, (3 - g) % 4]
            for f in (2, 1, 0):
                out = jnp.where(group == f, turned[f, k, (f - g) % 4], out)
            made.append(out)
        return made

    def from_neighbours(near, h):
        rows = slice(16 * h, 16 * h + 16)
        faces = faces_of(near, h)
        facing = coef(cn, Q, 0, rows, lower)
        masks = [flag(facing < 0.5), flag((facing > 0.5) & (facing < 1.5)), flag(facing > 1.5)]
        blocks = []
        for q in range(Q):
            acc = coef(cn, q, 0, rows, lower) * faces[0]
            for p in range(1, Q):
                acc = acc + coef(cn, q, p, rows, lower) * faces[p]
            blocks.append([acc * m for m in masks])
        return product(blocks, wu[512:896, :])

    def from_inside(xs, h):
        rows = slice(16 * h, 16 * h + 16)
        xp = paired(xs)
        blocks = []
        for q in range(Q):
            row = list(mix_star(xs, xp, q, rows))
            for lanes in (lower, upper):
                acc = coef(co, q, 0, rows, lanes) * xs[0]
                for p in range(1, Q):
                    acc = acc + coef(co, q, p, rows, lanes) * xs[p]
                row.append(acc)
            blocks.append(row)
        return product(blocks, wu[0:512, :])

    make_table(first)
    pl.semaphore_wait(barrier, 1 + n_off)
    started = exchange(send1, recv1, 0)

    near1[...] = dot(gather_loc[...], rhs[...])
    wait(9, 10)
    spread(own8, bh_own, co, 256)
    wait(13, 14, 15)
    nbr8[81, 0:4, :] = orient[...].astype(F32)
    spread(nbr8, bh_nbr, cn, 128)
    wait(11, 12, 16, 17)
    for d in range(4):
        w = sv[min(d, 2)]
        wu32[64 * d : 64 * d + M, 0:M] = w
        wu32[64 * d : 64 * d + M, 64 : 64 + M] = w
        w = fm[d]
        wu32[256 + 64 * d : 256 + 64 * d + M, 0:M] = w
        wu32[256 + 64 * d : 256 + 64 * d + M, 64 : 64 + M] = w
    for f in range(4):
        face = lift[:, f, :]
        for o in range(3):
            w = lax.dot_general(
                turn[o],
                face,
                (((1,), (0,)), ((), ())),
                precision=lax.Precision.HIGHEST,
                preferred_element_type=F32,
            )
            start = 512 + 128 * o + 32 * f
            wu32[start : start + J, 0:M] = w
            wu32[start : start + J, 64 : 64 + M] = w
    u_hi, u_lo = split2(wu32[...])
    wu[:, 0:128] = u_hi
    wu[:, 128:256] = u_lo

    inside = from_inside([first[q, 0:16, :] for q in range(Q)], 0)
    for q in range(Q):
        half[q] = state0[q, 0:16, :] + inside[16 * q : 16 * q + 16]
    inside = from_inside([first[q, 16:32, :] + second[q, 16:32, :] for q in range(Q)], 1)
    for q in range(Q):
        part[q, 16:32, :] = state0[q, 16:32, :] + inside[16 * q : 16 * q + 16]

    near1[...] = near1[...] + arrived(started, recv1)
    outside = from_neighbours(
        lambda f, k: near1[32 * f : 32 * f + 16, 128 * k : 128 * k + 128], 0
    )
    for q in range(Q):
        x = half[q] + outside[16 * q : 16 * q + 16]
        x = jnp.where(is_fine, x, state0[q, 0:16, :])
        half[q] = x
        term[q, 0:16, :] = x
        later[q, 0:16, :] = early[0] * x
        later[q, 16:32, :] = second[q, 16:32, :]
    predict(1, [(later, early)])
    for q in range(Q):
        later[q, 0:16, :] = jnp.where(is_fine, later[q, 0:16, :], second[q, 0:16, :])

    make_table(later)
    started = exchange(send2, recv2, 1)

    for f in range(4):
        top = slice(32 * f, 32 * f + 16)
        for k in range(3):
            lanes = slice(128 * k, 128 * k + 128)
            near1[top, lanes] = jnp.where(is_fine, 0.0, near1[top, lanes])
    near1[...] = near1[...] + dot(gather_loc[...], rhs[...])
    inside = from_inside(
        [
            jnp.where(is_fine, later[q, 0:16, :], first[q, 0:16, :] + second[q, 0:16, :])
            for q in range(Q)
        ],
        0,
    )
    for q in range(Q):
        part[q, 0:16, :] = half[q] + inside[16 * q : 16 * q + 16]
    wait(18, 19)
    unperm = dot_nt(flag(iota((32, 32), 0) == iota((32, 32), 1)).astype(BF16), perm).astype(BF16)
    unperm3 = jnp.concatenate([unperm, unperm, unperm], axis=1)
    offset = (fault * n_off + off) * E
    source_hot = flag(iota((32, 16), 0) + offset == src_elem[...]).astype(BF16)
    source_hot3 = jnp.concatenate([source_hot] * 3, axis=1)

    near1[...] = near1[...] + arrived(started, recv2)
    for h in range(2):
        outside = from_neighbours(
            lambda f, k: near1[
                32 * f + 16 * h : 32 * f + 16 * h + 16, 128 * k : 128 * k + 128
            ],
            h,
        )
        for q in range(Q):
            rows = slice(16 * h, 16 * h + 16)
            part[q, rows, :] = part[q, rows, :] + outside[16 * q : 16 * q + 16]
    for q in range(Q):
        made = dot(unperm3, jnp.concatenate(split3(part[q]), axis=0))
        added = dot(source_hot3, jnp.concatenate(split3(src_term[q]), axis=0))
        out_ref[q] = made[:, 0:M] + added


def on_device(
    modal_state,
    star_mats,
    flux_local,
    flux_nbr,
    stiff_time,
    stiff_vol,
    flux_minus,
    face_proj,
    face_turn,
    face_lift,
    cluster,
    send_elem,
    send_face,
    nbr_index,
    orientation,
    source_elem,
    source_term,
):
    n_fault = lax.axis_size("fault")
    n_off = lax.axis_size("off")
    inputs = [
        jnp.transpose(modal_state, (0, 2, 1)),
        jnp.transpose(star_mats, (1, 2, 0, 3)).reshape(81, 3, E),
        jnp.transpose(flux_local, (1, 2, 0, 3)).reshape(81, 4, E),
        jnp.transpose(flux_nbr, (1, 2, 0, 3)).reshape(81, 4, E),
        stiff_time,
        stiff_vol,
        flux_minus,
        jnp.transpose(face_proj, (2, 0, 1)),
        face_turn,
        jnp.transpose(face_lift, (1, 0, 2)),
        cluster.reshape(1, E),
        send_elem.reshape(1, 72),
        send_face.reshape(1, 72),
        nbr_index,
        orientation,
        source_elem.reshape(1, 16),
        jnp.transpose(source_term, (1, 0, 2)),
        *spread_tables(),
    ]
    own = {1: (84, 8, E), 2: (84, 8, E), 3: (84, 8, E)}
    held = [pltpu.VMEM(own.get(i, x.shape), x.dtype) for i, x in enumerate(inputs)]
    scratch = [
        *held,
        pltpu.VMEM((4, 21, E, 256), F32),
        pltpu.VMEM((Q, 5, E, 128), F32),
        pltpu.VMEM((4, 21, E, 256), F32),
        pltpu.VMEM((4, 21, E, 128), F32),
        pltpu.VMEM((21 * E, 256), BF16),
        pltpu.VMEM((256, 128), F32),
        pltpu.VMEM((256, 256), BF16),
        pltpu.VMEM((896, 128), F32),
        pltpu.VMEM((896, 256), BF16),
        pltpu.VMEM((512, 256), F32),
        pltpu.VMEM((512, 256), BF16),
        pltpu.VMEM((512, 256), BF16),
        pltpu.VMEM((Q, E, 128), F32),
        pltpu.VMEM((Q, E, 128), F32),
        pltpu.VMEM((Q, E, 128), F32),
        pltpu.VMEM((Q, E, 128), F32),
        pltpu.VMEM((Q, FINE, 128), F32),
        pltpu.VMEM((Q, E, 128), F32),
        pltpu.VMEM((Q, E, 128), F32),
        pltpu.VMEM((128, 384), F32),
        pltpu.VMEM((128, 256), BF16),
        pltpu.VMEM((128, 256), BF16),
        pltpu.VMEM((96, 256), BF16),
        pltpu.VMEM((256, 384), BF16),
        pltpu.VMEM((288, 128), F32),
        pltpu.VMEM((288, 128), F32),
        pltpu.VMEM((6, 48, 128), F32),
        pltpu.VMEM((6, 48, 128), F32),
        pltpu.SemaphoreType.DMA((len(inputs),)),
        pltpu.SemaphoreType.DMA((2, 5)),
        pltpu.SemaphoreType.DMA((2, 5)),
    ]
    made = pl.pallas_call(
        functools.partial(kernel, n_fault, n_off),
        out_shape=jax.ShapeDtypeStruct((Q, E, M), F32),
        in_specs=[pl.BlockSpec(memory_space=pl.ANY)] * len(inputs),
        out_specs=pl.BlockSpec(memory_space=pltpu.VMEM),
        scratch_shapes=scratch,
        compiler_params=pltpu.CompilerParams(
            collective_id=0, has_side_effects=True, vmem_limit_bytes=56 << 20
        ),
    )(*inputs)
    return jnp.transpose(made, (0, 2, 1))


def solution(mesh):
    in_specs = (
        P(None, None, ("fault", "off")),
        P(None, None, None, ("fault", "off")),
        P(None, None, None, ("fault", "off")),
        P(None, None, None, ("fault", "off")),
        P(),
        P(),
        P(),
        P(),
        P(),
        P(),
        P(("fault", "off")),
        P("fault", "off", None),
        P("fault", "off", None),
        P(None, ("fault", "off")),
        P(None, ("fault", "off")),
        P(),
        P(),
    )
    out_specs = P(None, None, ("fault", "off"))
    return jax.shard_map(
        on_device, mesh=mesh, in_specs=in_specs, out_specs=out_specs, check_vma=False
    )
```

profile of v0, /device:TPU:2, one launch (start us, length us, event | category | flops | bytes accessed | tf_op | source)
XLA Modules:
  0.0 32.9 jit_solution(7528419900031604279)
XLA Ops:
  0.0 31.3 %shard_map.190 = f32[9,32,56]{2,1,0:T(8,128)} custom-call(f32[9,32,56]{2,1,0:T(8,128)} %bitcast.22, f32[81,3,32]{2,1,0:T(4,128)} %bitcast.19, f32[81,4,32]{2,1,0:T(4,128)} %bitcast.20, f32[81,4,32]{2,1,0:T(4,128)} %bitcast.21, f32[3,56,56]{2,1,0:T(8,128)} %st_h.1, f32[3,56,56]{2,1,0:T(8,128)} %sv_h.1, f32[4,56,56]{2,1,0:T(8,128)} %fm_h.1, ...), custom_call_target="tpu_custom_call" | custom-call | tf_op jit(solution)/shard_map/pallas_call | solution.py:671
  31.3 1.6 %copy.22 = f32[9,56,32]{1,2,0:T(8,128)} copy(f32[9,56,32]{1,2,0:T(8,128)} %bitcast.18) | data formatting | bytes 129024
where the time goes:
time: 33 us; the launch traced here: 32.9 us
  Pallas kernels  31.3 us (95%)
  local copies, waits for them, and re-layouts  1.58 us (5%)
    pallas_call x1, Pallas kernels, on_device(): pl.pallas_call(functools.partial(kernel, n_fault, n_off), out_shape=jax.S...  31.3 us
    unnamed x1, local copies, waits for them, and re-layouts  1.58 us

commit v1 on v0

--- a/solution.py
+++ b/solution.py
@@ -63,10 +63,11 @@
 
     def table(pattern):
         width = pattern.shape[1]
-        out = np.zeros((4, 2, 4, 4, 8, width), np.float32)
+        out = np.zeros((2, 4, 4, 8, 4, width), np.float32)
         for i in range(4):
-            out[i, :, :, i, :4, :] = pattern
-        return out.reshape(4, 256, width)
+            out[:, :, i, :4, i, :] = pattern
+        out = out.reshape(256, 2, 2 * width)
+        return np.ascontiguousarray(out.transpose(1, 0, 2))
 
     return [jnp.asarray(table(t), BF16) for t in (star, own, nbr)]
 
@@ -90,11 +91,11 @@
     index_h,
     orient_h,
     src_elem_h,
-    src_term_h,
     bh_star_h,
     bh_own_h,
     bh_nbr_h,
-    out_ref,
+    part,
+    hot_ref,
     modal,
     star8,
     own8,
@@ -111,7 +112,6 @@
     index,
     orient,
     src_elem,
-    src_term,
     bh_star,
     bh_own,
     bh_nbr,
@@ -122,6 +122,8 @@
     spread_lhs,
     wt32,
     wt,
+    mixed_hi,
+    mixed_lo,
     wu32,
     wu,
     pw32,
@@ -133,7 +135,6 @@
     second,
     half,
     later,
-    part,
     near1,
     gather_loc,
     gather_rem,
@@ -175,7 +176,6 @@
         (turn_h, turn),
         (lift_h, lift),
         (src_elem_h, src_elem),
-        (src_term_h, src_term),
     ]
     copies = []
     for i, (src, dst) in enumerate(pairs):
@@ -193,7 +193,6 @@
             device_id_type=MESH,
         )
 
-    low_half = iota((16, 128), 1) < 64
 
     wt32[...] = jnp.zeros_like(wt32)
     wu32[...] = jnp.zeros_like(wu32)
@@ -220,11 +219,42 @@
     lane128 = iota((128, 128), 1)
     perm_big = flag(((row128 >> 5) == (lane128 >> 5)) & ((row128 & 31) == pos)).astype(BF16)
 
+    wait(6, 7)
+    wanted = send_face[...] * E + send_elem[...]
+    out_hot = flag(iota((128, 72), 0) == wanted).astype(BF16)
+    r = iota((96, 72), 0)
+    s = iota((96, 72), 1)
+    k_in = r & 15
+    slot_of = jnp.where(r < 32, r, jnp.where(k_in < 10, 32 + 10 * ((r >> 4) - 2) + k_in, -1))
+    picked = dot_nt(flag(slot_of == s).astype(BF16), out_hot).astype(BF16)
+    picked = dot_nt(picked, perm_big).astype(BF16)
+    gather_out[:, 0:128] = picked
+    gather_out[:, 128:256] = picked
+
+    wait(4)
+    for d in range(4):
+        w = st[min(d, 2)]
+        wt32[64 * d : 64 * d + M, 0:M] = w
+        wt32[64 * d : 64 * d + M, 64 : 64 + M] = w
+    w_hi, w_lo = split2(wt32[...])
+    wt[:, 0:128] = w_hi
+    wt[:, 128:256] = w_lo
+
+    wait(8)
+    for f in range(4):
+        face = proj[:, f, :]
+        for g in range(4):
+            start = 128 * f + 32 * g
+            pw32[start : start + J, 64 * g : 64 * g + M] = face
+    p_hi, p_lo = split2(pw32[...])
+    pw_hi[...] = p_hi
+    pw_lo[...] = p_lo
+
     def spread(rows, table, out, width):
-        flat = rows[...].reshape(84 * 8, 32)
+        flat = jnp.transpose(rows[...].reshape(84 * 8, 32))
         hi, lo = split2(flat)
-        g_hi = dot_nt(perm, hi).astype(BF16)
-        g_lo = dot_nt(perm, lo).astype(BF16)
+        g_hi = dot(perm, hi).astype(BF16)
+        g_lo = dot(perm, lo).astype(BF16)
         lane = iota((32, 128), 1)
         for tile in range(6):
             hi_t = g_hi[:, 128 * tile : 128 * tile + 128] if tile < 5 else None
@@ -240,10 +270,12 @@
                 spread_lhs[32 * chunk : 32 * chunk + 32, 128:256] = lo_t * keep
 
         def step(i, carry):
-            out[i] = dot(spread_lhs[...], table[i]).reshape(21, 32, width)
+            made = dot(spread_lhs[...], table[i])
+            out[2 * i] = made[:, 0:width].reshape(21, 32, width)
+            out[2 * i + 1] = made[:, width : 2 * width].reshape(21, 32, width)
             return carry
 
-        lax.fori_loop(0, 4, step, 0)
+        lax.fori_loop(0, 2, step, 0)
 
     wait(1, 2)
     spread(star8, bh_star, cs, 256)
@@ -261,15 +293,6 @@
             a = coef(cs, q, 2 * pair, whole, upper)
             b = coef(cs, q, 2 * pair + 1, whole, upper) if pair < 4 else 0.0
             cs2[q, pair] = jnp.where(low32, a, b)
-
-    wait(4)
-    for d in range(4):
-        w = st[min(d, 2)]
-        wt32[64 * d : 64 * d + M, 0:M] = w
-        wt32[64 * d : 64 * d + M, 64 : 64 + M] = w
-    w_hi, w_lo = split2(wt32[...])
-    wt[:, 0:128] = w_hi
-    wt[:, 128:256] = w_lo
 
     wait(3)
     term[...] = jnp.zeros_like(term)
@@ -287,7 +310,7 @@
         second[q] = late[0] * moved
 
     def paired(xs):
-        return [jnp.where(low_half, xs[2 * i], xs[2 * i + 1]) for i in range(4)] + [xs[8]]
+        return [jnp.where(iota(xs[0].shape, 1) < 64, xs[2 * i], xs[2 * i + 1]) for i in range(4)] + [xs[8]]
 
     def mix_star(xs, xp, q, rows):
         y01 = coef(cs, q, 0, rows, lower) * xs[0]
@@ -298,15 +321,24 @@
             y2 = y2 + cs2[q, i, rows, :] * xp[i]
         return y01, y2
 
+    def cut(blocks):
+        his, los = [], []
+        for i in range(len(blocks[0])):
+            column = [row[i] for row in blocks]
+            if column[0].shape[0] % 16:
+                column.append(jnp.zeros_like(column[0]))
+            hi, lo = split2(jnp.concatenate(column, axis=0))
+            his.append(hi)
+            los.append(lo)
+        return jnp.concatenate(his, axis=1), jnp.concatenate(los, axis=1)
+
+    def contract(hi, lo, weights):
+        both = dot(hi, weights)
+        extra = dot(lo, weights[:, 0:128])
+        return both[:, 0:128] + both[:, 128:256] + extra
+
     def product(blocks, weights):
-        his, los = [], []
-        for row in blocks:
-            cut = [split2(b) for b in row]
-            his.append(jnp.concatenate([c[0] for c in cut], axis=1))
-            los.append(jnp.concatenate([c[1] for c in cut], axis=1))
-        both = dot(jnp.concatenate(his, axis=0), weights)
-        extra = dot(jnp.concatenate(los, axis=0), weights[:, 0:128])
-        return both[:, 0:128] + both[:, 128:256] + extra
+        return contract(*cut(blocks), weights)
 
     def series_weight(k, values):
         w = jnp.float32(values[TERMS - 1])
@@ -314,63 +346,48 @@
             w = jnp.where(k == i, jnp.float32(values[i]), w)
         return w
 
-    def predict(halves, sums):
+    def predict(size, streams, sums):
+        filled = (Q * size + 15) // 16 * 16
+
+        def mix(stream):
+            rows = slice(size * stream, size * stream + size)
+            xs = [term[p, rows, :] for p in range(Q)]
+            xp = paired(xs)
+            hi, lo = cut([list(mix_star(xs, xp, q, rows)) for q in range(Q)])
+            mixed_hi[stream, 0:filled, :] = hi
+            mixed_lo[stream, 0:filled, :] = lo
+
+        def expand(stream, k):
+            rows = slice(size * stream, size * stream + size)
+            made = contract(mixed_hi[stream, 0:filled, :], mixed_lo[stream, 0:filled, :], wt[...])
+            for q in range(Q):
+                x = made[size * q : size * q + size]
+                term[q, rows, :] = x
+                for ref, values in sums:
+                    ref[q, rows, :] = ref[q, rows, :] + series_weight(k, values) * x
+
         def step(k, carry):
-            for h in range(halves):
-                rows = slice(16 * h, 16 * h + 16)
-                xs = [term[p, rows, :] for p in range(Q)]
-                xp = paired(xs)
-                blocks = [list(mix_star(xs, xp, q, rows)) for q in range(Q)]
-                made = product(blocks, wt[...])
-                for q in range(Q):
-                    x = made[16 * q : 16 * q + 16]
-                    term[q, rows, :] = x
-                    for ref, values in sums:
-                        ref[q, rows, :] = ref[q, rows, :] + series_weight(k, values) * x
+            expand(0, k)
+            mix(1)
+            expand(1, k)
+            mix(0)
             return carry
 
-        lax.fori_loop(1, TERMS, step, 0)
-
-    predict(2, [(first, early), (second, late)])
-
-    wait(5, 6, 7)
-    tab = iota((128, 32), 0)
-    slot = tab & 15
-    ghost = jnp.where(
-        tab < 32,
-        128 + tab,
-        jnp.where((slot < 10) & (tab < 96), 160 + 10 * ((tab >> 4) - 2) + slot, -1),
-    )
-    for f in range(4):
-        want = index[f : f + 1, :]
-        loc = dot_nt(perm, flag(tab == want).astype(BF16)).astype(BF16)
-        loc = dot_nt(loc, perm_big).astype(BF16)
-        rem = dot_nt(perm, flag(ghost == want).astype(BF16)).astype(BF16)
-        rows = slice(32 * f, 32 * f + 32)
-        gather_loc[rows, 0:128] = loc
-        gather_loc[rows, 128:256] = loc
-        gather_rem[rows, 0:128] = rem
-        gather_rem[rows, 128:256] = rem
-    wanted = send_face[...] * E + send_elem[...]
-    out_hot = flag(iota((128, 72), 0) == wanted).astype(BF16)
-    r = iota((96, 72), 0)
-    s = iota((96, 72), 1)
-    k_in = r & 15
-    slot_of = jnp.where(r < 32, r, jnp.where(k_in < 10, 32 + 10 * ((r >> 4) - 2) + k_in, -1))
-    picked = dot_nt(flag(slot_of == s).astype(BF16), out_hot).astype(BF16)
-    picked = dot_nt(picked, perm_big).astype(BF16)
-    gather_out[:, 0:128] = picked
-    gather_out[:, 128:256] = picked
-
-    wait(8)
-    for f in range(4):
-        face = proj[:, f, :]
-        for g in range(4):
-            start = 128 * f + 32 * g
-            pw32[start : start + J, 64 * g : 64 * g + M] = face
-    p_hi, p_lo = split2(pw32[...])
-    pw_hi[...] = p_hi
-    pw_lo[...] = p_lo
+        def lone(k, carry):
+            mix(0)
+            expand(0, k)
+            return carry
+
+        if streams == 1:
+            lax.fori_loop(1, TERMS, lone, 0)
+            return
+        mix(0)
+        lax.fori_loop(1, TERMS - 1, step, 0)
+        expand(0, TERMS - 1)
+        mix(1)
+        expand(1, TERMS - 1)
+
+    predict(16, 2, [(first, early), (second, late)])
 
     def make_table(integral):
         rows = []
@@ -400,6 +417,19 @@
                     16 * a : 16 * a + 16, 128 * k : 128 * k + 128
                 ]
         started = []
+        for step in (2, 1, 3):
+            to = lax.rem(off + step, n_off)
+            started.append(
+                pltpu.make_async_remote_copy(
+                    src_ref=sent.at[pl.ds(pl.multiple_of(96 + 48 * to, 8), 32), :],
+                    dst_ref=received.at[2 + off, pl.ds(0, 32), :],
+                    send_sem=send_sems.at[turn_no, 1 + step],
+                    recv_sem=recv_sems.at[turn_no, 1 + step],
+                    device_id={"off": to},
+                    device_id_type=MESH,
+                )
+            )
+            started[-1].start()
         for a, device in enumerate([{"fault": below}, {"fault": above}]):
             started.append(
                 pltpu.make_async_remote_copy(
@@ -408,19 +438,6 @@
                     send_sem=send_sems.at[turn_no, a],
                     recv_sem=recv_sems.at[turn_no, 1 - a],
                     device_id=device,
-                    device_id_type=MESH,
-                )
-            )
-            started[-1].start()
-        for step in range(1, n_off):
-            to = lax.rem(off + step, n_off)
-            started.append(
-                pltpu.make_async_remote_copy(
-                    src_ref=sent.at[pl.ds(pl.multiple_of(96 + 48 * to, 8), 32), :],
-                    dst_ref=received.at[2 + off, pl.ds(0, 32), :],
-                    send_sem=send_sems.at[turn_no, 1 + step],
-                    recv_sem=recv_sems.at[turn_no, 1 + step],
-                    device_id={"off": to},
                     device_id_type=MESH,
                 )
             )
@@ -496,6 +513,24 @@
     pl.semaphore_wait(barrier, 1 + n_off)
     started = exchange(send1, recv1, 0)
 
+    wait(5)
+    tab = iota((128, 32), 0)
+    slot = tab & 15
+    ghost = jnp.where(
+        tab < 32,
+        128 + tab,
+        jnp.where((slot < 10) & (tab < 96), 160 + 10 * ((tab >> 4) - 2) + slot, -1),
+    )
+    for f in range(4):
+        want = index[f : f + 1, :]
+        loc = dot_nt(perm, flag(tab == want).astype(BF16)).astype(BF16)
+        loc = dot_nt(loc, perm_big).astype(BF16)
+        rem = dot_nt(perm, flag(ghost == want).astype(BF16)).astype(BF16)
+        rows = slice(32 * f, 32 * f + 32)
+        gather_loc[rows, 0:128] = loc
+        gather_loc[rows, 128:256] = loc
+        gather_rem[rows, 0:128] = rem
+        gather_rem[rows, 128:256] = rem
     near1[...] = dot(gather_loc[...], rhs[...])
     wait(9, 10)
     spread(own8, bh_own, co, 256)
@@ -545,7 +580,7 @@
         term[q, 0:16, :] = x
         later[q, 0:16, :] = early[0] * x
         later[q, 16:32, :] = second[q, 16:32, :]
-    predict(1, [(later, early)])
+    predict(16, 1, [(later, early)])
     for q in range(Q):
         later[q, 0:16, :] = jnp.where(is_fine, later[q, 0:16, :], second[q, 0:16, :])
 
@@ -567,7 +602,7 @@
     )
     for q in range(Q):
         part[q, 0:16, :] = half[q] + inside[16 * q : 16 * q + 16]
-    wait(18, 19)
+    wait(18)
     unperm = dot_nt(flag(iota((32, 32), 0) == iota((32, 32), 1)).astype(BF16), perm).astype(BF16)
     unperm3 = jnp.concatenate([unperm, unperm, unperm], axis=1)
     offset = (fault * n_off + off) * E
@@ -585,10 +620,15 @@
         for q in range(Q):
             rows = slice(16 * h, 16 * h + 16)
             part[q, rows, :] = part[q, rows, :] + outside[16 * q : 16 * q + 16]
-    for q in range(Q):
-        made = dot(unperm3, jnp.concatenate(split3(part[q]), axis=0))
-        added = dot(source_hot3, jnp.concatenate(split3(src_term[q]), axis=0))
-        out_ref[q] = made[:, 0:M] + added
+    hot_ref[:, 0:96] = unperm3
+    hot_ref[:, 96:144] = source_hot3
+
+
+def finish(part, hot, src_term, out_ref):
+    for q in range(Q):
+        moved = jnp.concatenate(split3(part[q][:, 0:M]), axis=0)
+        added = jnp.concatenate(split3(src_term[q]), axis=0)
+        out_ref[q] = dot(hot[:, 0:96], moved) + dot(hot[:, 96:144], added)
 
 
 def on_device(
@@ -629,7 +669,6 @@
         nbr_index,
         orientation,
         source_elem.reshape(1, 16),
-        jnp.transpose(source_term, (1, 0, 2)),
         *spread_tables(),
     ]
     own = {1: (84, 8, E), 2: (84, 8, E), 3: (84, 8, E)}
@@ -643,6 +682,8 @@
         pltpu.VMEM((21 * E, 256), BF16),
         pltpu.VMEM((256, 128), F32),
         pltpu.VMEM((256, 256), BF16),
+        pltpu.VMEM((2, 144, 256), BF16),
+        pltpu.VMEM((2, 144, 256), BF16),
         pltpu.VMEM((896, 128), F32),
         pltpu.VMEM((896, 256), BF16),
         pltpu.VMEM((512, 256), F32),
@@ -653,7 +694,6 @@
         pltpu.VMEM((Q, E, 128), F32),
         pltpu.VMEM((Q, E, 128), F32),
         pltpu.VMEM((Q, FINE, 128), F32),
-        pltpu.VMEM((Q, E, 128), F32),
         pltpu.VMEM((Q, E, 128), F32),
         pltpu.VMEM((128, 384), F32),
         pltpu.VMEM((128, 256), BF16),
@@ -668,16 +708,25 @@
         pltpu.SemaphoreType.DMA((2, 5)),
         pltpu.SemaphoreType.DMA((2, 5)),
     ]
-    made = pl.pallas_call(
+    part, hot = pl.pallas_call(
         functools.partial(kernel, n_fault, n_off),
-        out_shape=jax.ShapeDtypeStruct((Q, E, M), F32),
+        out_shape=[
+            jax.ShapeDtypeStruct((Q, E, 128), F32),
+            jax.ShapeDtypeStruct((E, 144), BF16),
+        ],
         in_specs=[pl.BlockSpec(memory_space=pl.ANY)] * len(inputs),
-        out_specs=pl.BlockSpec(memory_space=pltpu.VMEM),
+        out_specs=[pl.BlockSpec(memory_space=pltpu.VMEM)] * 2,
         scratch_shapes=scratch,
         compiler_params=pltpu.CompilerParams(
             collective_id=0, has_side_effects=True, vmem_limit_bytes=56 << 20
         ),
     )(*inputs)
+    made = pl.pallas_call(
+        finish,
+        out_shape=jax.ShapeDtypeStruct((Q, E, M), F32),
+        in_specs=[pl.BlockSpec(memory_space=pltpu.VMEM)] * 3,
+        out_specs=pl.BlockSpec(memory_space=pltpu.VMEM),
+    )(part, hot, jnp.transpose(source_term, (1, 0, 2)))
     return jnp.transpose(made, (0, 2, 1))
 
 

time: 33 us -> 31.9 us (0.967)
  local copies, waits for them, and re-layouts: 1.58 us -> 0 us
  Pallas kernels: 31.3 us -> 31.7 us
    unnamed x1 -> x0, local copies, waits for them, and re-layouts: 1.58 us -> none
    pallas_call x1 -> x2, Pallas kernels: 31.3 us -> 31.7 us  [the longest x1 29.8 us: on_device(): pl.pallas_call(functools.partial(kernel, n_fault, n_off), out_shape=[jax....]
where the time goes in v1:
time: 31.9 us; the launch traced here: 31.7 us
  Pallas kernels  31.7 us (99%)
    pallas_call x1, Pallas kernels, on_device(): pl.pallas_call(functools.partial(kernel, n_fault, n_off), out_shape=[jax....  29.8 us
    pallas_call x1, Pallas kernels, on_device(): pl.pallas_call(finish, out_shape=jax.ShapeDtypeStruct((Q, E, M), F32), in...  1.9 us

profile of v1, /device:TPU:2, one launch (start us, length us, event | category | flops | bytes accessed | tf_op | source)
XLA Modules:
  0.0 31.7 jit_solution(10064067029986640728)
XLA Ops:
  0.0 29.8 %shard_map.190 = (f32[9,32,128]{2,1,0:T(8,128)}, bf16[32,144]{1,0:T(8,128)(2,1)}) custom-call(f32[9,32,56]{2,1,0:T(8,128)} %bitcast.21, f32[81,3,32]{2,1,0:T(4,128)} %bitcast.18, f32[81,4,32]{2,1,0:T(4,128)} %bitcast.19, f32[81,4,32]{2,1,0:T(4,128)} %bitcast.20, f32[3,56,56]{2,1,0:T(8,128)} %st_h.1, f32[3,56,56]{2,1,0:T(8,128)} %sv_h.1, f32[4,56,56]{2,1,0:T(8,128)} %fm_h.1, ...), custom_call_target="tpu_custom_call" | custom-call | tf_op jit(solution)/shard_map/pallas_call | solution.py:711
  29.8 1.9 %shard_map.191 = f32[9,32,56]{2,1,0:T(8,128)} custom-call(f32[9,32,128]{2,1,0:T(8,128)} %get-tuple-element.7.part, bf16[32,144]{1,0:T(8,128)(2,1)} %get-tuple-element.8.hot, f32[9,16,56]{2,1,0:T(8,128)} %bitcast.22), custom_call_target="tpu_custom_call" | custom-call | tf_op jit(solution)/shard_map/pallas_call | solution.py:724

commit v2 on v1

--- a/solution.py
+++ b/solution.py
@@ -246,7 +246,7 @@
         for g in range(4):
             start = 128 * f + 32 * g
             pw32[start : start + J, 64 * g : 64 * g + M] = face
-    p_hi, p_lo = split2(pw32[...])
+    p_hi, p_lo = split2(jnp.transpose(pw32[...]))
     pw_hi[...] = p_hi
     pw_lo[...] = p_lo
 
@@ -275,7 +275,8 @@
             out[2 * i + 1] = made[:, width : 2 * width].reshape(21, 32, width)
             return carry
 
-        lax.fori_loop(0, 2, step, 0)
+        step(0, 0)
+        step(1, 0)
 
     wait(1, 2)
     spread(star8, bh_star, cs, 256)
@@ -401,7 +402,8 @@
             jnp.concatenate([jnp.where(low32, xs[8], 0.0), jnp.zeros((32, 128), F32)], axis=1)
         )
         hi, lo = split2(jnp.concatenate(rows, axis=0))
-        faced = dot_nt(hi, pw_hi[...]) + dot_nt(hi, pw_lo[...]) + dot_nt(lo, pw_hi[...])
+        both = dot(jnp.concatenate([hi, lo], axis=0), pw_hi[...])
+        faced = both[0:96] + both[96:192] + dot(hi, pw_lo[...])
         for k in range(3):
             for f in range(4):
                 t_hi, t_lo = split2(faced[32 * k : 32 * k + 32, 128 * f : 128 * f + 128])
@@ -411,11 +413,15 @@
 
     def exchange(sent, received, turn_no):
         outgoing = dot(gather_out[...], rhs[...])
-        for a in range(6):
-            for k in range(3):
-                sent[pl.ds(48 * a + k, 16, stride=3), :] = outgoing[
-                    16 * a : 16 * a + 16, 128 * k : 128 * k + 128
-                ]
+
+        def store(slots):
+            for a in slots:
+                for k in range(3):
+                    sent[pl.ds(48 * a + k, 16, stride=3), :] = outgoing[
+                        16 * a : 16 * a + 16, 128 * k : 128 * k + 128
+                    ]
+
+        store(range(2, 6))
         started = []
         for step in (2, 1, 3):
             to = lax.rem(off + step, n_off)
@@ -430,6 +436,7 @@
                 )
             )
             started[-1].start()
+        store(range(2))
         for a, device in enumerate([{"fault": below}, {"fault": above}]):
             started.append(
                 pltpu.make_async_remote_copy(
@@ -626,9 +633,8 @@
 
 def finish(part, hot, src_term, out_ref):
     for q in range(Q):
-        moved = jnp.concatenate(split3(part[q][:, 0:M]), axis=0)
-        added = jnp.concatenate(split3(src_term[q]), axis=0)
-        out_ref[q] = dot(hot[:, 0:96], moved) + dot(hot[:, 96:144], added)
+        terms = [*split3(part[q][:, 0:M]), *split3(src_term[q])]
+        out_ref[q] = dot(hot[...], jnp.concatenate(terms, axis=0))
 
 
 def on_device(
@@ -687,8 +693,8 @@
         pltpu.VMEM((896, 128), F32),
         pltpu.VMEM((896, 256), BF16),
         pltpu.VMEM((512, 256), F32),
-        pltpu.VMEM((512, 256), BF16),
-        pltpu.VMEM((512, 256), BF16),
+        pltpu.VMEM((256, 512), BF16),
+        pltpu.VMEM((256, 512), BF16),
         pltpu.VMEM((Q, E, 128), F32),
         pltpu.VMEM((Q, E, 128), F32),
         pltpu.VMEM((Q, E, 128), F32),

time: 31.9 us -> 31.5 us (0.987)
  Pallas kernels: 31.7 us -> 31.3 us
    pallas_call x1, Pallas kernels: 29.8 us -> 29.5 us  [on_device(): pl.pallas_call(functools.partial(kernel, n_fault, n_off), out_shape=[jax....]
where the time goes in v2:
time: 31.5 us; the launch traced here: 31.4 us
  Pallas kernels  31.3 us (99%)
    pallas_call x1, Pallas kernels, on_device(): pl.pallas_call(functools.partial(kernel, n_fault, n_off), out_shape=[jax....  29.5 us
    pallas_call x1, Pallas kernels, on_device(): pl.pallas_call(finish, out_shape=jax.ShapeDtypeStruct((Q, E, M), F32), in...  1.87 us

profile of v2, /device:TPU:2, one launch (start us, length us, event | category | flops | bytes accessed | tf_op | source)
XLA Modules:
  0.0 31.4 jit_solution(14532305313408145307)
XLA Ops:
  0.0 29.5 %shard_map.190 = (f32[9,32,128]{2,1,0:T(8,128)}, bf16[32,144]{1,0:T(8,128)(2,1)}) custom-call(f32[9,32,56]{2,1,0:T(8,128)} %bitcast.21, f32[81,3,32]{2,1,0:T(4,128)} %bitcast.18, f32[81,4,32]{2,1,0:T(4,128)} %bitcast.19, f32[81,4,32]{2,1,0:T(4,128)} %bitcast.20, f32[3,56,56]{2,1,0:T(8,128)} %st_h.1, f32[3,56,56]{2,1,0:T(8,128)} %sv_h.1, f32[4,56,56]{2,1,0:T(8,128)} %fm_h.1, ...), custom_call_target="tpu_custom_call" | custom-call | tf_op jit(solution)/shard_map/pallas_call | solution.py:717
  29.5 1.9 %shard_map.191 = f32[9,32,56]{2,1,0:T(8,128)} custom-call(f32[9,32,128]{2,1,0:T(8,128)} %get-tuple-element.7.part, bf16[32,144]{1,0:T(8,128)(2,1)} %get-tuple-element.8.hot, f32[9,16,56]{2,1,0:T(8,128)} %bitcast.22), custom_call_target="tpu_custom_call" | custom-call | tf_op jit(solution)/shard_map/pallas_call | solution.py:730
